TPU v7x, 32 devices: a whole 2x2x4 slice. The times are simulated.
32 devices in a mesh: curve: 16 (over z, y, x), colour: 2 (over core).
Axes of the slice: x: 2, y: 2, z: 4, core: 2. Of those that a mesh axis runs over, the one named last changes fastest.
Arguments:
- vectors: float32 [128, 320, 128], P(('curve', 'colour')), may hold values from -6 to 6
- inverse_blocks: bfloat16 [128, 320, 320], P(('curve', 'colour'))
- face_jac: float32 [128, 6, 5, 5, 16], P(('curve', 'colour')), may hold values from -2.64 to 2.64
- volume_jac: float32 [128, 3, 5, 5, 64], P(('curve', 'colour')), may hold values from -2.5 to 2.5
- neighbour_kind: int32 [128, 6], P(('curve', 'colour')), may hold values from 0 to 3, as said below
- neighbour_slot: int32 [128, 6], P(('curve', 'colour')), may hold values from 0 to 23
- hanging_face: int32 [128, 6], P(('curve', 'colour')), may hold values from 0 to 4
- send_upward: int32 [32], P(('curve', 'colour')), may hold values from 0 to 23, as said below
- send_downward: int32 [32], P(('curve', 'colour')), may hold values from 0 to 23
Outputs:
- preconditioned: float32 [128, 320, 128], P(('curve', 'colour'))
Inputs may be any that keep to these rules, and one draw needn't show every extreme that they name: `neighbour_kind`: 0 marks a boundary face, 1 a neighbour on the same device, 2 one on the device before, 3 one on the device after. On every device, for each i < 1, the face named by send_upward entry i has kind 2 and neighbour_slot mod 1 equal to i, and the face named by send_downward entry i has kind 3 and neighbour_slot mod 1 equal to i. The 2 faces that one device names in send_upward and send_downward are all different.
All inputs are finite; a program needn't handle non-finite values.
Results may differ from a plain program's by a relative error of at most 0.0003.
Values sent between devices are 32-bit elements; how exact they have to be, the bound alone decides.
A program may use at most 192 MiB of HBM per device.

v0:
```python
import functools

import jax
import jax.numpy as jnp
import numpy as np
from jax import lax
from jax.experimental import pallas as pl
from jax.experimental.pallas import tpu as pltpu
from jax.sharding import PartitionSpec as P

NP = 4
F32 = jnp.float32
BF16 = jnp.bfloat16
AXES = ("curve", "colour")


def edge_points(edge_count):
    return -np.cos(np.pi * np.arange(edge_count) / (edge_count - 1))


def lagrange_values(edge_nodes, points):
    values = np.ones((len(points), len(edge_nodes)))
    for j in range(len(edge_nodes)):
        for m in range(len(edge_nodes)):
            if m != j:
                values[:, j] = (
                    values[:, j] * (points - edge_nodes[m]) / (edge_nodes[j] - edge_nodes[m])
                )
    return values


def lagrange_slopes(edge_nodes):
    point_count = len(edge_nodes)
    slopes = np.zeros((point_count, point_count))
    for i in range(point_count):
        for j in range(point_count):
            for m in range(point_count):
                if m != j:
                    product = 1.0 / (edge_nodes[j] - edge_nodes[m])
                    for k in range(point_count):
                        if k != j and k != m:
                            product = (
                                product
                                * (edge_nodes[i] - edge_nodes[k])
                                / (edge_nodes[j] - edge_nodes[k])
                            )
                    slopes[i, j] = slopes[i, j] + product
    return slopes


def mortar_tiles():
    edge_nodes = edge_points(NP)
    halves = [
        lagrange_values(edge_nodes, (edge_nodes - 1.0) / 2.0),
        lagrange_values(edge_nodes, (edge_nodes + 1.0) / 2.0),
    ]
    tables = [np.eye(NP * NP)]
    for q in range(4):
        tables.append(np.kron(halves[q // 2], halves[q % 2]))
    return np.tile(np.stack(tables), (1, 5, 15)).astype(np.float32)


def slope_tiles():
    d = 0.25 * lagrange_slopes(edge_points(NP))
    e = np.eye(NP)
    maps = [np.kron(np.kron(d, e), e), np.kron(np.kron(e, d), e), np.kron(np.kron(e, e), d)]
    return np.tile(np.stack(maps), (1, 1, 5)).astype(np.float32)


def split(x):
    high = x.astype(BF16)
    return high, (x - high.astype(F32)).astype(BF16)


def mm(a, b):
    return jnp.dot(a, b, preferred_element_type=F32)


def product(a, b):
    ah, al = split(a)
    bh, bl = split(b)
    return mm(ah, bh) + mm(ah, bl) + mm(al, bh)


def face_values(x, s, tmp):
    last = NP - 1 if s % 2 else 0
    if s < 2:
        return jnp.concatenate([x[pl.ds(f * 64 + last * 16, 16), :] for f in range(5)], axis=0)
    if s < 4:
        for c in range(4):
            tmp[pl.ds(c, 20, stride=4), :] = x[pl.ds(last * 4 + c, 20, stride=16), :]
        return tmp[...]
    return x[pl.ds(last, 80, stride=4), :]


def lift_into(acc, s, value, tmp):
    last = NP - 1 if s % 2 else 0
    if s < 2:
        for f in range(5):
            acc[pl.ds(f * 64 + last * 16, 16), :] += value[f * 16 : f * 16 + 16]
    elif s < 4:
        tmp[...] = value
        for c in range(4):
            acc[pl.ds(last * 4 + c, 20, stride=16), :] += tmp[pl.ds(c, 20, stride=4), :]
    else:
        acc[pl.ds(last, 80, stride=4), :] += value


def stacked(t):
    high, low = split(t)
    return jnp.concatenate([high, low, high], axis=0)


def pick_kernel(up_ref, down_ref, u_ref, out_ref, traces, tmp):
    for k, which in enumerate((up_ref, down_ref)):
        owner = which[0] // 6
        mine = u_ref.at[owner]
        for s in range(6):
            traces[s] = face_values(mine, s, tmp.at[s])
        out_ref[k] = traces[which[0] % 6]


def local_kernel(
    kind_ref,
    slot_ref,
    hang_ref,
    up_ref,
    down_ref,
    u_ref,
    inv_ref,
    jac_ref,
    vjac_ref,
    near_ref,
    mortar_ref,
    slope_ref,
    fwd_ref,
    bwd_ref,
    res_ref,
    maps,
    table_u,
    table_f,
    table_b,
    image,
    lowered,
    solved,
    acc,
    tmp,
):
    elements = u_ref.shape[0]
    rows = elements * 6
    lane = lax.broadcasted_iota(jnp.int32, (80, 240), 1)
    eye = (
        lax.broadcasted_iota(jnp.int32, (80, 128), 0)
        == lax.broadcasted_iota(jnp.int32, (80, 128), 1)
    ).astype(F32)
    none = jnp.zeros((240, 128), BF16)
    unit = stacked(eye)

    for j in range(elements):
        for s in range(6):
            wide = jac_ref[j * 6 + s] * mortar_ref[hang_ref[j, s]]
            high = wide.astype(BF16).astype(F32)
            maps[j * 6 + s] = jnp.where(lane < 160, high, wide - high).astype(BF16)
            table_u[j * 6 + s] = stacked(face_values(u_ref.at[j], s, tmp.at[s]))
    table_u[rows] = stacked(near_ref[0])
    table_u[rows + 1] = stacked(near_ref[1])
    table_u[rows + 2] = none
    for g in range(2):
        table_f[rows, :, g * 128 : g * 128 + 128] = unit if g == 1 else none
        table_f[rows + 1, :, g * 128 : g * 128 + 128] = none
    for g in range(3):
        table_b[rows, :, g * 128 : g * 128 + 128] = unit if g == 2 else none
        table_b[rows + 1, :, g * 128 : g * 128 + 128] = none

    for j in range(elements):
        parts = []
        for f in range(5):
            part = slope_ref[0] * vjac_ref[j, 0, f : f + 1, :]
            for t in range(1, 3):
                part = part + slope_ref[t] * vjac_ref[j, t, f : f + 1, :]
            parts.append(part)
        volume = jnp.concatenate(parts, axis=0)
        image[j] = u_ref[j] + product(volume, u_ref[j])
        for s in range(6):
            kind, slot = kind_ref[j, s], slot_ref[j, s]
            row = jnp.where(
                kind == 1, slot, jnp.where(kind == 2, rows, jnp.where(kind == 3, rows + 1, rows + 2))
            )
            lift_into(image.at[j], s, mm(maps[j * 6 + s], table_u[row]), tmp.at[s])

    for j in range(elements):
        acc[0] = jnp.zeros((320, 128), F32)
        acc[1] = jnp.zeros((320, 128), F32)
        for s in range(6):
            kind, slot = kind_ref[j, s], slot_ref[j, s]
            local = (kind == 1) & (slot < 6 * j)
            row = jnp.where(local, slot, jnp.where(kind == 2, rows, rows + 1))
            value = mm(maps[j * 6 + s], table_f[row])
            for g in range(2):
                lift_into(acc.at[g], s, value[:, g * 128 : g * 128 + 128], tmp.at[s * 3 + g])
        high, low = split(jnp.concatenate([image[j] - acc[0], -acc[1]], axis=1))
        value = mm(inv_ref[j], high) + mm(inv_ref[j], low)
        for g in range(2):
            lowered[g, j] = value[:, g * 128 : g * 128 + 128]
            for s in range(6):
                table_f[j * 6 + s, :, g * 128 : g * 128 + 128] = stacked(
                    face_values(lowered.at[g, j], s, tmp.at[s * 3 + g])
                )
    out = table_f[up_ref[0]]
    out = out[:80].astype(F32) + out[80:160].astype(F32)
    fwd_ref[0] = out[:, :128]
    fwd_ref[1] = out[:, 128:]

    for p in range(elements):
        j = elements - 1 - p
        for g in range(3):
            acc[g] = jnp.zeros((320, 128), F32)
        for s in range(6):
            kind, slot = kind_ref[j, s], slot_ref[j, s]
            local = (kind == 1) & (slot >= 6 * (j + 1))
            row = jnp.where(local, slot, jnp.where(kind == 3, rows, rows + 1))
            value = mm(maps[j * 6 + s], table_b[row])
            for g in range(3):
                lift_into(acc.at[g], s, value[:, g * 128 : g * 128 + 128], tmp.at[s * 3 + g])
        high, low = split(jnp.concatenate([acc[g] for g in range(3)], axis=1))
        value = mm(inv_ref[j], high) + mm(inv_ref[j], low)
        for g in range(3):
            part = value[:, g * 128 : g * 128 + 128]
            solved[g, j] = lowered[g, j] - part if g < 2 else -part
            res_ref[j, :, g * 128 : g * 128 + 128] = solved[g, j]
            for s in range(6):
                table_b[j * 6 + s, :, g * 128 : g * 128 + 128] = stacked(
                    face_values(solved.at[g, j], s, tmp.at[s * 3 + g])
                )
    out = table_b[down_ref[0]]
    out = out[:80].astype(F32) + out[80:160].astype(F32)
    for g in range(3):
        bwd_ref[g] = out[:, g * 128 : g * 128 + 128]


def scan_rounds(count):
    first = min(3, max(count - 1, 1))
    rounds, cover = [list(range(1, first + 1))], first
    while cover < count - 1:
        radix = 4 if cover * 3 < count - 1 else (3 if cover * 2 < count - 1 else 2)
        rounds.append([cover * i for i in range(1, radix)])
        cover *= radix
    return rounds


def scan_kernel(
    curve_size,
    colour_size,
    fwd_ref,
    bwd_ref,
    res_ref,
    out_ref,
    state_f,
    state_m,
    state_c,
    recv_f,
    recv_m,
    recv_c,
    both,
    send_sems,
    recv_sems,
):
    count = curve_size * colour_size
    rounds = scan_rounds(count)
    width = max(len(r) for r in rounds)
    me = lax.axis_index("curve") * colour_size + lax.axis_index("colour")

    def at(offset):
        other = lax.rem(me + offset + count, count)
        return (other // colour_size, lax.rem(other, colour_size))

    barrier = pltpu.get_barrier_semaphore()
    greeted = 0
    for offset in sorted({o for r in rounds for o in r}):
        for signed, there in ((offset, me + offset < count), (-offset, me >= offset)):
            greeted = greeted + there.astype(jnp.int32)

            @pl.when(there)
            def _():
                pl.semaphore_signal(
                    barrier, inc=1, device_id=at(signed), device_id_type=pl.DeviceIdType.MESH
                )

    pl.semaphore_wait(barrier, greeted)

    def exchange(kind, k, i, upward, source, target):
        offset = rounds[k][i]
        has_to = me + offset < count if upward else me >= offset
        has_from = me >= offset if upward else me + offset < count
        copy = pltpu.make_async_remote_copy(
            src_ref=source,
            dst_ref=target,
            send_sem=send_sems.at[kind, k, i],
            recv_sem=recv_sems.at[kind, k, i],
            device_id=at(offset if upward else -offset),
            device_id_type=pl.DeviceIdType.MESH,
        )

        @pl.when(has_to)
        def _():
            copy.start()

        @pl.when(jnp.logical_not(has_from))
        def _():
            target[...] = jnp.zeros(target.shape, F32)

        return copy, has_to, has_from

    sent = []

    def arrive(copies):
        for copy, has_to, has_from in copies:
            sent.append((copy, has_to))

            @pl.when(has_from)
            def _(copy=copy):
                copy.wait_recv()

    def compose(first, second):
        value = product(first[1][:, :80], jnp.concatenate([second[0], second[1]], axis=1))
        return (first[0] + value[:, :128], value[:, 128:])

    state_f[0] = fwd_ref[...]
    state_m[0] = bwd_ref[2]
    for k, offsets in enumerate(rounds):
        final = k == len(rounds) - 1
        copies = []
        for i in range(len(offsets)):
            copies.append(exchange(0, k, i, True, state_f.at[k], recv_f.at[k, i]))
            copies.append(exchange(1, k, i, False, state_m.at[k], recv_m.at[k, i]))
        arrive(copies)
        chain = [(recv_f[k, i, 0], recv_f[k, i, 1]) for i in range(len(offsets))]
        chain_m = [recv_m[k, i] for i in range(len(offsets))]
        if k > 0:
            chain = [(state_f[k, 0], state_f[k, 1])] + chain
            chain_m = [state_m[k]] + chain_m
        total = chain[-1]
        for item in chain[-2::-1]:
            total = compose(item, total)
        state_f[k + 1, 0] = total[0]
        if not final:
            state_f[k + 1, 1] = total[1]
            total_m = chain_m[-1]
            for item in chain_m[-2::-1]:
                total_m = product(item[:, :80], total_m)
            state_m[k + 1] = total_m

    incoming = state_f[len(rounds), 0]
    both[...] = jnp.zeros(both.shape, F32)
    both[0:80] = incoming
    state_c[0] = bwd_ref[0] + product(bwd_ref[1][:, :80], incoming)
    for k, offsets in enumerate(rounds):
        copies = [
            exchange(2, k, i, False, state_c.at[k], recv_c.at[k, i]) for i in range(len(offsets))
        ]
        arrive(copies)
        chain = [(recv_c[k, i], recv_m.at[k, i]) for i in range(len(offsets))]
        if k > 0:
            chain = [(state_c[k], state_m.at[k])] + chain
        total = chain[-1][0]
        for value, factor in chain[-2::-1]:
            total = value + product(factor[...][:, :80], total)
        state_c[k + 1] = total
    both[128:208] = state_c[len(rounds)]

    high, low = split(both[...])
    for j in range(out_ref.shape[0]):
        wh, wl = split(res_ref[j, :, 128:384])
        out_ref[j] = res_ref[j, :, 0:128] + mm(wh, high) + mm(wh, low) + mm(wl, high)
    for copy, has_to in sent:

        @pl.when(has_to)
        def _(copy=copy):
            copy.wait_send()


def on_device(
    curve_size,
    colour_size,
    vectors,
    inverse_blocks,
    face_jac,
    volume_jac,
    neighbour_kind,
    neighbour_slot,
    hanging_face,
    send_upward,
    send_downward,
):
    elements = vectors.shape[0]
    rows = elements * 6
    count = curve_size * colour_size
    rounds = scan_rounds(count)
    width = max(len(r) for r in rounds)
    smem = pl.BlockSpec(memory_space=pltpu.SMEM)
    vmem = pl.BlockSpec(memory_space=pltpu.VMEM)
    limit = 56 * 1024 * 1024

    near = pl.pallas_call(
        pick_kernel,
        out_shape=jax.ShapeDtypeStruct((2, 80, 128), F32),
        in_specs=[smem, smem, vmem],
        out_specs=vmem,
        scratch_shapes=[pltpu.VMEM((6, 80, 128), F32), pltpu.VMEM((6, 80, 128), F32)],
        compiler_params=pltpu.CompilerParams(vmem_limit_bytes=limit),
        name="pick",
    )(send_upward, send_downward, vectors)
    below = lax.ppermute(near[0], AXES, [(i, i + 1) for i in range(count - 1)])
    above = lax.ppermute(near[1], AXES, [(i + 1, i) for i in range(count - 1)])

    jac_wide = jnp.transpose(face_jac, (0, 1, 2, 4, 3)).reshape(rows, 80, 5)
    jac_wide = jnp.tile(jnp.repeat(jac_wide, 16, axis=2), (1, 1, 3))
    fwd, bwd, res = pl.pallas_call(
        local_kernel,
        out_shape=(
            jax.ShapeDtypeStruct((2, 80, 128), F32),
            jax.ShapeDtypeStruct((3, 80, 128), F32),
            jax.ShapeDtypeStruct((elements, 320, 384), F32),
        ),
        in_specs=[smem] * 5 + [vmem] * 7,
        out_specs=(vmem, vmem, vmem),
        scratch_shapes=[
            pltpu.VMEM((rows, 80, 240), BF16),
            pltpu.VMEM((rows + 3, 240, 128), BF16),
            pltpu.VMEM((rows + 2, 240, 256), BF16),
            pltpu.VMEM((rows + 2, 240, 384), BF16),
            pltpu.VMEM((elements, 320, 128), F32),
            pltpu.VMEM((2, elements, 320, 128), F32),
            pltpu.VMEM((3, elements, 320, 128), F32),
            pltpu.VMEM((3, 320, 128), F32),
            pltpu.VMEM((18, 80, 128), F32),
        ],
        compiler_params=pltpu.CompilerParams(vmem_limit_bytes=limit),
        name="local",
    )(
        neighbour_kind,
        neighbour_slot,
        hanging_face,
        send_upward,
        send_downward,
        vectors,
        inverse_blocks,
        jac_wide,
        volume_jac.reshape(elements, 3, 5, 320),
        jnp.stack([below, above]),
        jnp.asarray(mortar_tiles()),
        jnp.asarray(slope_tiles()),
    )
    depth = len(rounds)
    return pl.pallas_call(
        functools.partial(scan_kernel, curve_size, colour_size),
        out_shape=jax.ShapeDtypeStruct(vectors.shape, F32),
        in_specs=[vmem] * 3,
        out_specs=vmem,
        scratch_shapes=[
            pltpu.VMEM((depth + 1, 2, 80, 128), F32),
            pltpu.VMEM((depth + 1, 80, 128), F32),
            pltpu.VMEM((depth + 1, 80, 128), F32),
            pltpu.VMEM((depth, width, 2, 80, 128), F32),
            pltpu.VMEM((depth, width, 80, 128), F32),
            pltpu.VMEM((depth, width, 80, 128), F32),
            pltpu.VMEM((256, 128), F32),
            pltpu.SemaphoreType.DMA((3, depth, width)),
            pltpu.SemaphoreType.DMA((3, depth, width)),
        ],
        compiler_params=pltpu.CompilerParams(
            vmem_limit_bytes=limit, collective_id=0, has_side_effects=True
        ),
        name="scan",
    )(fwd, bwd, res)


def solution(mesh):
    split_first = lambda rank: P(AXES, *([None] * (rank - 1)))
    return jax.shard_map(
        functools.partial(on_device, mesh.shape["curve"], mesh.shape["colour"]),
        mesh=mesh,
        in_specs=tuple(split_first(r) for r in (3, 3, 5, 5, 2, 2, 2, 1, 1)),
        out_specs=split_first(3),
        check_vma=False,
    )
```

profile of v0, /device:TPU:0, one launch (start us, length us, event | category | flops | bytes accessed | tf_op | source)
XLA Modules:
  0.0 73.6 jit_solution(412195549067115993)
XLA Ops:
  1.3 1.8 %pick.1 = f32[2,80,128]{2,1,0:T(8,128)} custom-call(s32[1]{0:T(128)S(6)} %copy.23.up_ref, s32[1]{0:T(128)S(6)} %copy.24.down_ref, f32[4,320,128]{2,1,0:T(8,128)} %u_ref.3), custom_call_target="tpu_custom_call" | custom-call | tf_op jit(solution)/shard_map/pick/pallas_call | solution.py:404
  3.1 0.8 %slice_bitcast_fusion.1 = (f32[80,128]{1,0:T(8,128)S(1)}, f32[80,128]{1,0:T(8,128)S(1)}) fusion(f32[2,80,128]{2,1,0:T(8,128)} %pick.1), kind=kLoop, calls=%fused_computation.2 | loop fusion | bytes 163840 | tf_op jit(solution)/shard_map/squeeze | solution.py:413
  3.9 1.3 %collective-permute-start.1 = (f32[80,128]{1,0:T(8,128)S(1)}, f32[80,128]{1,0:T(8,128)S(1)}, u32[]{:S(2)}, u32[]{:S(2)}) collective-permute-start(f32[80,128]{1,0:T(8,128)S(1)} %get-tuple-element.12), channel_id=1, source_target_pairs={{1,0},{2,1},{3,2},{4,3},{5,4},{6,5},{7,6},{8,7},{9,8},{10,9},{11,1... | collective-permute-start | bytes 122888 | tf_op jit(solution)/shard_map/ppermute | solution.py:414
  5.2 3.0 %collective-permute-start = (f32[80,128]{1,0:T(8,128)S(1)}, f32[80,128]{1,0:T(8,128)S(1)}, u32[]{:S(2)}, u32[]{:S(2)}) collective-permute-start(f32[80,128]{1,0:T(8,128)S(1)} %get-tuple-element.11), channel_id=1, source_target_pairs={{0,1},{1,2},{2,3},{3,4},{4,5},{5,6},{6,7},{7,8},{8,9},{9,10},{10,1... | collective-permute-start | bytes 122888 | tf_op jit(solution)/shard_map/ppermute | solution.py:413
  8.3 1.0 %copy.18 = f32[4,6,5,16,5]{3,2,4,1,0:T(8,128)S(1)} copy(f32[4,6,5,16,5]{3,0,4,2,1:T(4,128)} %bitcast.13) | data formatting | bytes 76800 | tf_op jit(solution)/shard_map/reshape | solution.py:416
  9.3 0.1 reshape.12
  9.4 0.1 broadcast_in_dim.3
  9.5 0.2 tile.11
  9.7 0.0 copy-start
  9.7 2.1 %copy.16.jac_ref = f32[24,80,240]{2,1,0:T(8,128)} copy(f32[24,80,240]{1,2,0:T(8,128)S(1)} %bitcast.11) | data formatting | bytes 3686400 | tf_op jit(solution)/shard_map/tile | solution.py:417
  11.8 0.0 copy-done
  11.9 0.7 %reshape.13.vjac_ref = f32[4,3,5,320]{3,2,1,0:T(8,128)} reshape(f32[4,3,5,5,64]{4,3,2,1,0:T(8,128)S(1)} %copy.19) | data formatting | bytes 153600 | tf_op jit(solution)/shard_map/reshape | solution.py:449
  12.6 0.0 collective-permute-done.1
  12.6 0.0 collective-permute-done
  12.6 0.6 pad_maximum_fusion.near_ref
  13.2 13.5 %local.1 = (f32[2,80,128]{2,1,0:T(8,128)}, f32[3,80,128]{2,1,0:T(8,128)}, f32[4,320,384]{2,1,0:T(8,128)}) custom-call(s32[4,6]{1,0:T(4,128)} %kind_ref.1, s32[4,6]{1,0:T(4,128)} %slot_ref.1, s32[4,6]{1,0:T(4,128)} %hang_ref.1, s32[1]{0:T(128)S(6)} %copy.23.up_ref, s32[1]{0:T(128)S(6)} %copy.24.down_ref, f32[4,320,128]{2,1,0:T(8,128)} %u_ref.3, ...), custom_call_target="tpu_custom_call" | custom-call | tf_op jit(solution)/shard_map/local/pallas_call | solution.py:418
  26.8 44.8 %scan.1 = f32[4,320,128]{2,1,0:T(8,128)} custom-call(f32[2,80,128]{2,1,0:T(8,128)} %get-tuple-element.8.fwd_ref, f32[3,80,128]{2,1,0:T(8,128)} %get-tuple-element.9.bwd_ref, f32[4,320,384]{2,1,0:T(8,128)} %get-tuple-element.10.res_ref), custom_call_target="tpu_custom_call" | custom-call | tf_op jit(solution)/shard_map/scan/pallas_call | solution.py:455
  71.6 2.0 %copy.25 = f32[4,320,128]{2,1,0:T(8,128)} copy(f32[4,320,128]{2,1,0:T(8,128)} %scan.1) | data formatting | bytes 1310720
  (1 shorter events, 0.0 us)
Async XLA Ops:
  3.9 8.7 %collective-permute-start.1 = (f32[80,128]{1,0:T(8,128)S(1)}, f32[80,128]{1,0:T(8,128)S(1)}, u32[]{:S(2)}, u32[]{:S(2)}) collective-permute-start(f32[80,128]{1,0:T(8,128)S(1)} %get-tuple-element.12), channel_id=1, source_target_pairs={{1,0},{2,1},{3,2},{4,3},{5,4},{6,5},{7,6},{8,7},{9,8},{10,9},{11,1... | collective-permute-start | bytes 122888 | tf_op jit(solution)/shard_map/ppermute | solution.py:414
  5.2 7.4 %collective-permute-start = (f32[80,128]{1,0:T(8,128)S(1)}, f32[80,128]{1,0:T(8,128)S(1)}, u32[]{:S(2)}, u32[]{:S(2)}) collective-permute-start(f32[80,128]{1,0:T(8,128)S(1)} %get-tuple-element.11), channel_id=1, source_target_pairs={{0,1},{1,2},{2,3},{3,4},{4,5},{5,6},{6,7},{7,8},{8,9},{9,10},{10,1... | collective-permute-start | bytes 122888 | tf_op jit(solution)/shard_map/ppermute | solution.py:413
  9.7 2.1 %copy-start = (f32[4,3,5,5,64]{4,0,3,2,1:T(4,128)S(1)}, f32[4,3,5,5,64]{4,0,3,2,1:T(4,128)}, u32[]{:S(2)}) copy-start(f32[4,3,5,5,64]{4,0,3,2,1:T(4,128)} %param.14) | copy-start | bytes 230404
where the time goes:
time: 74.7 us; the launch traced here: 73.6 us
  Pallas kernels  60.2 us (81%)
  local copies, waits for them, and re-layouts  7.07 us (9%)
  starting transfers between devices  4.31 us (6%)
  between operations  1.36 us (2%)
    pallas_call x1, Pallas kernels, on_device(): pl.pallas_call(functools.partial(scan_kernel, curve_size, colour_size), o...  44.8 us
    pallas_call x1, Pallas kernels, on_device(): pl.pallas_call(local_kernel, out_shape=(jax.ShapeDtypeStruct((2, 80, 128)...  13.5 us
    ppermute x1, starting transfers between devices, on_device(): below = lax.ppermute(near[0], AXES, [(i, i + 1) for i in range(count - 1)])  3.03 us
    another operation x2, local copies, waits for them, and re-layouts, on_device(): jac_wide = jnp.tile(jnp.repeat(jac_wide, 16, axis=2), (1, 1, 3))  2.29 us
    unnamed x3, local copies, waits for them, and re-layouts  1.97 us
    pallas_call x1, Pallas kernels, on_device(): pl.pallas_call(pick_kernel, out_shape=jax.ShapeDtypeStruct((2, 80, 128),...  1.83 us
  transfers between devices with their start and end apart: 2, of which 0 were waited for; matrix products, arithmetic and copies ran while one was open for 6% of the time, Pallas kernels for 0%

commit v1 on v0

v1 whole, which is shorter than its diff:
```python
import functools

import jax
import jax.numpy as jnp
import numpy as np
from jax import lax
from jax.experimental import pallas as pl
from jax.experimental.pallas import tpu as pltpu
from jax.sharding import PartitionSpec as P

NP = 4
F32 = jnp.float32
BF16 = jnp.bfloat16
AXES = ("curve", "colour")


def edge_points(edge_count):
    return -np.cos(np.pi * np.arange(edge_count) / (edge_count - 1))


def lagrange_values(edge_nodes, points):
    values = np.ones((len(points), len(edge_nodes)))
    for j in range(len(edge_nodes)):
        for m in range(len(edge_nodes)):
            if m != j:
                values[:, j] = (
                    values[:, j] * (points - edge_nodes[m]) / (edge_nodes[j] - edge_nodes[m])
                )
    return values


def lagrange_slopes(edge_nodes):
    point_count = len(edge_nodes)
    slopes = np.zeros((point_count, point_count))
    for i in range(point_count):
        for j in range(point_count):
            for m in range(point_count):
                if m != j:
                    product = 1.0 / (edge_nodes[j] - edge_nodes[m])
                    for k in range(point_count):
                        if k != j and k != m:
                            product = (
                                product
                                * (edge_nodes[i] - edge_nodes[k])
                                / (edge_nodes[j] - edge_nodes[k])
                            )
                    slopes[i, j] = slopes[i, j] + product
    return slopes


def mortar_tiles():
    edge_nodes = edge_points(NP)
    halves = [
        lagrange_values(edge_nodes, (edge_nodes - 1.0) / 2.0),
        lagrange_values(edge_nodes, (edge_nodes + 1.0) / 2.0),
    ]
    tables = [np.eye(NP * NP)]
    for q in range(4):
        tables.append(np.kron(halves[q // 2], halves[q % 2]))
    return np.tile(np.stack(tables), (1, 5, 15)).astype(np.float32)


def slope_tiles():
    d = 0.25 * lagrange_slopes(edge_points(NP))
    e = np.eye(NP)
    maps = [np.kron(np.kron(d, e), e), np.kron(np.kron(e, d), e), np.kron(np.kron(e, e), d)]
    return np.tile(np.stack(maps), (1, 1, 5)).astype(np.float32)


def split(x):
    high = x.astype(BF16)
    return high, (x - high.astype(F32)).astype(BF16)


def mm(a, b):
    return jnp.dot(a, b, preferred_element_type=F32)


def product(a, b):
    ah, al = split(a)
    bh, bl = split(b)
    return mm(ah, bh) + mm(ah, bl) + mm(al, bh)


def face_values(x, s, tmp):
    last = NP - 1 if s % 2 else 0
    if s < 2:
        return jnp.concatenate([x[pl.ds(f * 64 + last * 16, 16), :] for f in range(5)], axis=0)
    if s < 4:
        for c in range(4):
            tmp[pl.ds(c, 20, stride=4), :] = x[pl.ds(last * 4 + c, 20, stride=16), :]
        return tmp[...]
    return x[pl.ds(last, 80, stride=4), :]


def lift_into(acc, s, value, tmp):
    last = NP - 1 if s % 2 else 0
    if s < 2:
        for f in range(5):
            acc[pl.ds(f * 64 + last * 16, 16), :] += value[f * 16 : f * 16 + 16]
    elif s < 4:
        tmp[...] = value
        for c in range(4):
            acc[pl.ds(last * 4 + c, 20, stride=16), :] += tmp[pl.ds(c, 20, stride=4), :]
    else:
        acc[pl.ds(last, 80, stride=4), :] += value


def stacked(t):
    high, low = split(t)
    return jnp.concatenate([high, low, high], axis=0)


def scan_rounds(count):
    if count == 1:
        return []
    first = min(3, count - 1)
    rounds, cover = [list(range(1, first + 1))], first
    while cover < count - 1:
        radix = 4 if cover * 3 < count - 1 else (3 if cover * 2 < count - 1 else 2)
        rounds.append([cover * i for i in range(1, radix)])
        cover *= radix
    return rounds


def group_size(count):
    return next(size for size in (8, 4, 2, 1) if count % size == 0)


def kernel(
    curve_size,
    colour_size,
    kind_ref,
    slot_ref,
    hang_ref,
    up_ref,
    down_ref,
    u_ref,
    inv_ref,
    jac_ref,
    vjac_ref,
    mortar_ref,
    slope_ref,
    out_ref,
    maps,
    traces,
    leaving,
    near,
    table_u,
    table_wf,
    table_wb,
    table_y,
    table_z,
    image,
    wide_f,
    wide_b,
    lowered,
    solved,
    acc,
    tmp,
    group_m,
    group_v,
    factors,
    state_m,
    recv_m,
    state_v,
    recv_v,
    both,
    near_send,
    near_recv,
    group_send,
    group_recv,
    chain_send,
    chain_recv,
):
    elements = u_ref.shape[0]
    rows = elements * 6
    count = curve_size * colour_size
    size = group_size(count)
    rounds = scan_rounds(count // size)
    me = lax.axis_index("curve") * colour_size + lax.axis_index("colour")
    place = lax.rem(me, size)
    first = me - place

    def coordinates(other):
        other = lax.rem(other + count, count)
        return (other // colour_size, lax.rem(other, colour_size))

    barrier = pltpu.get_barrier_semaphore()
    greeted = jnp.int32(size - 1)

    def greet(other):
        pl.semaphore_signal(
            barrier, inc=1, device_id=coordinates(other), device_id_type=pl.DeviceIdType.MESH
        )

    def peer(i):
        return first + lax.rem(place + i, size)

    for i in range(1, size):
        greet(peer(i))
    distant = [
        (me + 1, (place == size - 1) & (me + 1 < count)),
        (me - 1, (place == 0) & (me > 0)),
    ]
    for offset in sorted({o for r in rounds for o in r}):
        if offset * size > 1:
            distant.append((me + offset * size, me + offset * size < count))
            distant.append((me - offset * size, me >= offset * size))
    for other, there in distant:
        greeted = greeted + there.astype(jnp.int32)

        @pl.when(there)
        def _(other=other):
            greet(other)

    sent = []

    def remote(source, target, send, recv, other, has_to, has_from):
        copy = pltpu.make_async_remote_copy(
            src_ref=source,
            dst_ref=target,
            send_sem=send,
            recv_sem=recv,
            device_id=coordinates(other),
            device_id_type=pl.DeviceIdType.MESH,
        )

        @pl.when(has_to)
        def _():
            copy.start()

        @pl.when(jnp.logical_not(has_from))
        def _():
            target[...] = jnp.zeros(target.shape, F32)

        sent.append((copy, has_to))
        return copy, has_from

    def arrive(copies):
        for copy, has_from in copies:

            @pl.when(has_from)
            def _(copy=copy):
                copy.wait_recv()

    lane = lax.broadcasted_iota(jnp.int32, (80, 240), 1)
    eye = (
        lax.broadcasted_iota(jnp.int32, (80, 128), 0)
        == lax.broadcasted_iota(jnp.int32, (80, 128), 1)
    ).astype(F32)
    none = jnp.zeros((240, 128), BF16)
    spread = (
        lax.rem(lax.broadcasted_iota(jnp.int32, (5, 240), 1), 80) // 16
        == lax.broadcasted_iota(jnp.int32, (5, 240), 0)
    ).astype(BF16)
    for j in range(elements):
        for s in range(6):
            t = face_values(u_ref.at[j], s, tmp.at[s])
            traces[j * 6 + s] = t
            table_u[j * 6 + s] = stacked(t)
    table_u[rows] = none
    leaving[0] = traces[up_ref[0]]
    leaving[1] = traces[down_ref[0]]
    pl.semaphore_wait(barrier, greeted)
    after, before = me + 1 < count, me > 0
    near_copies = [
        remote(leaving.at[0], near.at[0], near_send.at[0], near_recv.at[0], me + 1, after, before),
        remote(leaving.at[1], near.at[1], near_send.at[1], near_recv.at[1], me - 1, before, after),
    ]
    for j in range(elements):
        for s in range(6):
            high, low = split(jac_ref[j * 6 + s])
            wide = (mm(high, spread) + mm(low, spread)) * mortar_ref[hang_ref[j, s]]
            high = wide.astype(BF16).astype(F32)
            maps[j * 6 + s] = jnp.where(lane < 160, high, wide - high).astype(BF16)

    def step(j, backward, table, remote_row, empty_row, accs, tmps, own, dests):
        groups = len(dests)
        for g in range(groups):
            acc[accs + g] = jnp.zeros((320, 128), F32)
        for s in range(6):
            kind, slot = kind_ref[j, s], slot_ref[j, s]
            inside = slot >= 6 * (j + 1) if backward else slot < 6 * j
            row = jnp.where(kind == (3 if backward else 2), remote_row, empty_row)
            row = jnp.where((kind == 1) & inside, slot, row)
            value = mm(maps[j * 6 + s], table[row])
            for g in range(groups):
                lift_into(
                    acc.at[accs + g], s, value[:, g * 128 : g * 128 + 128], tmp.at[tmps + 6 * g + s]
                )
        if backward:
            right = [acc[accs + g] for g in range(groups)]
        else:
            right = [own[g] - acc[accs + g] for g in range(groups)]
        high, low = split(jnp.concatenate(right, axis=1) if groups > 1 else right[0])
        value = mm(inv_ref[j], high) + mm(inv_ref[j], low)
        for g in range(groups):
            part = value[:, g * 128 : g * 128 + 128]
            dests[g][...] = own[g] - part if backward else part
            for s in range(6):
                table[j * 6 + s, :, g * 128 : g * 128 + 128] = stacked(
                    face_values(dests[g], s, tmp.at[tmps + 6 * g + s])
                )

    def outgoing(table, which):
        out = table[which]
        return out[:80].astype(F32) + out[80:160].astype(F32)

    def share(buffer, kind):
        copies = []
        for i in range(1, size):
            copy = pltpu.make_async_remote_copy(
                src_ref=buffer.at[place],
                dst_ref=buffer.at[place],
                send_sem=group_send.at[kind, i],
                recv_sem=group_recv.at[kind, place],
                device_id=coordinates(peer(i)),
                device_id_type=pl.DeviceIdType.MESH,
            )
            copy.start()
            sent.append((copy, None))
        for i in range(1, size):
            other = lax.rem(place + i, size)
            copies.append(
                pltpu.make_async_remote_copy(
                    src_ref=buffer.at[other],
                    dst_ref=buffer.at[other],
                    send_sem=group_send.at[kind, i],
                    recv_sem=group_recv.at[kind, other],
                    device_id=coordinates(peer(i)),
                    device_id_type=pl.DeviceIdType.MESH,
                )
            )
        return copies

    unit = stacked(eye)
    for table in (table_wf, table_wb):
        table[rows] = unit
        table[rows + 1] = none
    zero = jnp.zeros((320, 128), F32)
    for p in range(elements):
        q = elements - 1 - p
        step(p, False, table_wf, rows, rows + 1, 0, 0, [zero], [wide_f.at[p]])
        step(q, True, table_wb, rows, rows + 1, 1, 6, [zero], [wide_b.at[q]])
    group_m[0, place] = outgoing(table_wf, up_ref[0])
    group_m[1, place] = outgoing(table_wb, down_ref[0])
    shared_m = [share(group_m.at[0], 0), share(group_m.at[1], 1)]

    arrive(near_copies)
    table_u[rows + 1] = stacked(near[0])
    table_u[rows + 2] = stacked(near[1])
    for j in range(elements):
        parts = []
        for f in range(5):
            part = slope_ref[0] * vjac_ref[j, 0, f : f + 1, :]
            for t in range(1, 3):
                part = part + slope_ref[t] * vjac_ref[j, t, f : f + 1, :]
            parts.append(part)
        volume = jnp.concatenate(parts, axis=0)
        image[j] = u_ref[j] + product(volume, u_ref[j])
        for s in range(6):
            kind, slot = kind_ref[j, s], slot_ref[j, s]
            row = jnp.where(kind == 1, slot, jnp.where(kind == 0, rows, rows + kind - 1))
            lift_into(image.at[j], s, mm(maps[j * 6 + s], table_u[row]), tmp.at[s])
    table_y[rows] = none
    for j in range(elements):
        step(j, False, table_y, rows, rows, 0, 0, [image[j]], [lowered.at[j]])
    group_v[0, place] = outgoing(table_y, up_ref[0])
    shared_f = share(group_v.at[0], 2)

    for copies in shared_m:
        for copy in copies:
            copy.wait_recv()
    chains = [jnp.concatenate([eye, eye], axis=0)] * 2
    for step_index in range(size):
        for way in range(2):
            e = step_index if way else size - 1 - step_index
            mine = place < e if way else place > e
            high, low = split(jnp.concatenate([jnp.where(mine, chains[way][:80], 0.0), chains[way][80:]], 0))
            factors[way, e, 0] = high
            factors[way, e, 1] = low
            m = group_m[way, e]
            mh, ml = split(m)
            full = chains[way][:, :80]
            ch, cl = split(full)
            following = mm(ch, mh) + mm(ch, ml) + mm(cl, mh)
            chains[way] = jnp.concatenate([jnp.where(mine, following[:80], eye), following[80:]], 0)
    enter = [chain[:80] for chain in chains]
    state_m[0, 0] = chains[0][80:]
    state_m[1, 0] = chains[1][80:]

    def pass_on(way, k, i, source, target, kind):
        offset = rounds[k][i] * size
        below, above = me >= offset, me + offset < count
        return remote(
            source,
            target,
            chain_send.at[kind, k, i],
            chain_recv.at[kind, k, i],
            me - offset if way else me + offset,
            below if way else above,
            above if way else below,
        )

    def start_m(k):
        return [
            pass_on(way, k, i, state_m.at[way, k], recv_m.at[way, k, i], way)
            for i in range(len(rounds[k]))
            for way in range(2)
        ]

    pending = start_m(0) if rounds else []

    table_z[rows, :, 0:128] = none
    table_z[rows, :, 128:256] = none
    for p in range(elements):
        q = elements - 1 - p
        step(
            q,
            True,
            table_z,
            rows,
            rows,
            0,
            0,
            [lowered[q], wide_f[q]],
            [solved.at[0, q], solved.at[1, q]],
        )
    back = outgoing(table_z, down_ref[0])

    for k in range(len(rounds)):
        arrive(pending)
        if k + 1 < len(rounds):
            for way in range(2):
                factor = [recv_m[way, k, i] for i in range(len(rounds[k]))]
                if k > 0:
                    factor = [state_m[way, k]] + factor
                total = factor[-1]
                for item in factor[-2::-1]:
                    total = product(item[:, :80], total)
                state_m[way, k + 1] = total
            pending = start_m(k + 1)

    def scan(way, copies):
        for copy in copies:
            copy.wait_recv()
        total = jnp.zeros((160, 128), F32)
        for e in range(size):
            high, low = split(group_v[way, e])
            fh, fl = factors[way, e, 0][:, :80], factors[way, e, 1][:, :80]
            total = total + mm(fh, high) + mm(fh, low) + mm(fl, high)
        if not rounds:
            return total[:80]
        state_v[way, 0] = total[80:]
        for k, offsets in enumerate(rounds):
            arrive(
                [
                    pass_on(way, k, i, state_v.at[way, k], recv_v.at[way, k, i], 2 + way)
                    for i in range(len(offsets))
                ]
            )
            links = [(recv_v.at[way, k, i], recv_m.at[way, k, i]) for i in range(len(offsets))]
            if k > 0:
                links = [(state_v.at[way, k], state_m.at[way, k])] + links
            value = links[-1][0][...]
            for term, factor in links[-2::-1]:
                value = term[...] + product(factor[:, :80], value)
            state_v[way, k + 1] = value
        return total[:80] + product(enter[way][:, :80], state_v[way, len(rounds)])

    both[...] = jnp.zeros(both.shape, F32)
    incoming = scan(0, shared_f)
    group_v[1, place] = back[:, :128] + product(back[:, 128:208], incoming)
    shared_b = share(group_v.at[1], 3)
    both[0:80] = incoming
    both[128:208] = scan(1, shared_b)

    high, low = split(both[...])
    for j in range(elements):
        wh, wl = split(jnp.concatenate([solved[1, j], wide_b[j]], axis=1))
        out_ref[j] = solved[0, j] + mm(wh, high) + mm(wh, low) + mm(wl, high)
    for copy, has_to in sent:
        if has_to is None:
            copy.wait_send()
        else:

            @pl.when(has_to)
            def _(copy=copy):
                copy.wait_send()


def on_device(
    curve_size,
    colour_size,
    vectors,
    inverse_blocks,
    face_jac,
    volume_jac,
    neighbour_kind,
    neighbour_slot,
    hanging_face,
    send_upward,
    send_downward,
):
    elements = vectors.shape[0]
    rows = elements * 6
    count = curve_size * colour_size
    size = group_size(count)
    rounds = scan_rounds(count // size)
    depth = max(len(rounds), 1)
    width = max([len(r) for r in rounds] + [1])
    smem = pl.BlockSpec(memory_space=pltpu.SMEM)
    vmem = pl.BlockSpec(memory_space=pltpu.VMEM)
    face = (80, 128)
    return pl.pallas_call(
        functools.partial(kernel, curve_size, colour_size),
        out_shape=jax.ShapeDtypeStruct(vectors.shape, F32),
        in_specs=[smem] * 5 + [vmem] * 6,
        out_specs=vmem,
        scratch_shapes=[
            pltpu.VMEM((rows, 80, 240), BF16),
            pltpu.VMEM((rows,) + face, F32),
            pltpu.VMEM((2,) + face, F32),
            pltpu.VMEM((2,) + face, F32),
            pltpu.VMEM((rows + 3, 240, 128), BF16),
            pltpu.VMEM((rows + 2, 240, 128), BF16),
            pltpu.VMEM((rows + 2, 240, 128), BF16),
            pltpu.VMEM((rows + 1, 240, 128), BF16),
            pltpu.VMEM((rows + 1, 240, 256), BF16),
            pltpu.VMEM((elements, 320, 128), F32),
            pltpu.VMEM((elements, 320, 128), F32),
            pltpu.VMEM((elements, 320, 128), F32),
            pltpu.VMEM((elements, 320, 128), F32),
            pltpu.VMEM((2, elements, 320, 128), F32),
            pltpu.VMEM((2, 320, 128), F32),
            pltpu.VMEM((12,) + face, F32),
            pltpu.VMEM((2, size) + face, F32),
            pltpu.VMEM((2, size) + face, F32),
            pltpu.VMEM((2, size, 2, 160, 128), BF16),
            pltpu.VMEM((2, depth + 1) + face, F32),
            pltpu.VMEM((2, depth, width) + face, F32),
            pltpu.VMEM((2, depth + 1) + face, F32),
            pltpu.VMEM((2, depth, width) + face, F32),
            pltpu.VMEM((256, 128), F32),
            pltpu.SemaphoreType.DMA((2,)),
            pltpu.SemaphoreType.DMA((2,)),
            pltpu.SemaphoreType.DMA((4, size)),
            pltpu.SemaphoreType.DMA((4, size)),
            pltpu.SemaphoreType.DMA((4, depth, width)),
            pltpu.SemaphoreType.DMA((4, depth, width)),
        ],
        compiler_params=pltpu.CompilerParams(
            vmem_limit_bytes=56 * 1024 * 1024, collective_id=0, has_side_effects=True
        ),
        name="whole",
    )(
        neighbour_kind,
        neighbour_slot,
        hanging_face,
        send_upward,
        send_downward,
        vectors,
        inverse_blocks,
        jnp.transpose(face_jac, (0, 1, 2, 4, 3)).reshape(rows, 80, 5),
        volume_jac.reshape(elements, 3, 5, 320),
        jnp.asarray(mortar_tiles()),
        jnp.asarray(slope_tiles()),
    )


def solution(mesh):
    split_first = lambda rank: P(AXES, *([None] * (rank - 1)))
    return jax.shard_map(
        functools.partial(on_device, mesh.shape["curve"], mesh.shape["colour"]),
        mesh=mesh,
        in_specs=tuple(split_first(r) for r in (3, 3, 5, 5, 2, 2, 2, 1, 1)),
        out_specs=split_first(3),
        check_vma=False,
    )
```

time: 74.7 us -> 55.4 us (0.74); the launches traced: 73.6 us -> 55.1 us
  Pallas kernels: 60.2 us -> 48.4 us
  starting transfers between devices: 4.31 us -> 0 us
  local copies, waits for them, and re-layouts: 7.07 us -> 5.43 us
    pallas_call x3 -> x1, Pallas kernels: 60.2 us -> 48.4 us  [on_device(): pl.pallas_call(functools.partial(kernel, curve_size, colour_size), out_sh...]
    ppermute x2 -> x0, starting transfers between devices: 4.31 us -> none  [the longest x1 3.03 us: on_device(): below = lax.ppermute(near[0], AXES, [(i, i + 1) for i in range(count - 1)])]
    another operation x2 -> x0, local copies, waits for them, and re-layouts: 2.29 us -> none  [on_device(): jac_wide = jnp.tile(jnp.repeat(jac_wide, 16, axis=2), (1, 1, 3))]
    transpose x0 -> x1, local copies, waits for them, and re-layouts: none -> 1.72 us  [on_device(): jnp.transpose(face_jac, (0, 1, 2, 4, 3)).reshape(rows, 80, 5)]
    reshape x2 -> x0, local copies, waits for them, and re-layouts: 1.16 us -> none  [on_device(): jac_wide = jnp.transpose(face_jac, (0, 1, 2, 4, 3)).reshape(rows, 80, 5)]
    reshape x2, local copies, waits for them, and re-layouts: 0.78 us -> 1.74 us  [on_device(): volume_jac.reshape(elements, 3, 5, 320)]
    squeeze x1 -> x0, local copies, waits for them, and re-layouts: 0.8 us -> none  [on_device(): below = lax.ppermute(near[0], AXES, [(i, i + 1) for i in range(count - 1)])]
  transfers between devices with their start and end apart: 2 -> 0, of which waited for: 0 -> 0; matrix products, arithmetic and copies ran while one was open for 6% -> 0% of each run, Pallas kernels for 0% -> 0%
where the time goes in v1:
time: 55.4 us; the launch traced here: 55.1 us
  Pallas kernels  48.4 us (87%)
  local copies, waits for them, and re-layouts  5.43 us (10%)
  between operations  1.32 us (2%)
    pallas_call x1, Pallas kernels, on_device(): pl.pallas_call(functools.partial(kernel, curve_size, colour_size), out_sh...  48.4 us
    unnamed x3, local copies, waits for them, and re-layouts  1.97 us
    reshape x2, local copies, waits for them, and re-layouts, on_device(): volume_jac.reshape(elements, 3, 5, 320)  1.74 us
    transpose x1, local copies, waits for them, and re-layouts, on_device(): jnp.transpose(face_jac, (0, 1, 2, 4, 3)).reshape(rows, 80, 5)  1.72 us

profile of v1, /device:TPU:0, one launch (start us, length us, event | category | flops | bytes accessed | tf_op | source)
XLA Modules:
  0.0 55.1 jit_solution(12288892502972151376)
XLA Ops:
  1.3 0.0 copy-start
  1.3 1.0 %copy.17 = f32[4,3,5,5,64]{4,3,2,1,0:T(8,128)S(1)} copy(f32[4,3,5,5,64]{4,0,3,2,1:T(4,128)} %param.14) | data formatting | bytes 153600 | tf_op jit(solution)/shard_map/reshape | solution.py:566
  2.3 0.7 %reshape.8.vjac_ref = f32[4,3,5,320]{3,2,1,0:T(8,128)} reshape(f32[4,3,5,5,64]{4,3,2,1,0:T(8,128)S(1)} %copy.17) | data formatting | bytes 153600 | tf_op jit(solution)/shard_map/reshape | solution.py:566
  3.0 0.0 copy-done
  3.1 1.7 %copy.14 = f32[4,6,5,16,5]{4,3,2,1,0:T(8,128)} copy(f32[4,6,5,16,5]{3,0,4,2,1:T(4,128)S(1)} %bitcast.3) | data formatting | bytes 76800 | tf_op jit(solution)/shard_map/transpose | solution.py:565
  4.8 48.4 %whole.1 = f32[4,320,128]{2,1,0:T(8,128)} custom-call(s32[4,6]{1,0:T(4,128)} %kind_ref.1, s32[4,6]{1,0:T(4,128)} %slot_ref.1, s32[4,6]{1,0:T(4,128)} %hang_ref.1, s32[1]{0:T(128)S(6)} %copy.20.up_ref, s32[1]{0:T(128)S(6)} %copy.21.down_ref, f32[4,320,128]{2,1,0:T(8,128)} %u_ref.1, bf16[4,320,320]{2,1,0:T(8,128)(2,1)} %inv_ref.1, f32[24,80,5]{2,1,0:T(8,128)} %bitcast.2, ...), custom_call_target="tpu_custom_call" | custom-call | tf_op jit(solution)/shard_map/whole/pallas_call | solution.py:516
  53.2 2.0 %copy.22 = f32[4,320,128]{2,1,0:T(8,128)} copy(f32[4,320,128]{2,1,0:T(8,128)} %whole.1) | data formatting | bytes 1310720
Async XLA Ops:
  1.3 1.8 %copy-start = (f32[4,6,5,5,16]{4,0,3,2,1:T(4,128)S(1)}, f32[4,6,5,5,16]{4,0,3,2,1:T(4,128)}, u32[]{:S(2)}) copy-start(f32[4,6,5,5,16]{4,0,3,2,1:T(4,128)} %param.13) | copy-start | bytes 115204

commit v2 on v1

--- a/solution.py
+++ b/solution.py
@@ -340,12 +340,9 @@
         table[rows + 1] = none
     zero = jnp.zeros((320, 128), F32)
     for p in range(elements):
-        q = elements - 1 - p
         step(p, False, table_wf, rows, rows + 1, 0, 0, [zero], [wide_f.at[p]])
-        step(q, True, table_wb, rows, rows + 1, 1, 6, [zero], [wide_b.at[q]])
     group_m[0, place] = outgoing(table_wf, up_ref[0])
-    group_m[1, place] = outgoing(table_wb, down_ref[0])
-    shared_m = [share(group_m.at[0], 0), share(group_m.at[1], 1)]
+    shared_mf = share(group_m.at[0], 0)
 
     arrive(near_copies)
     table_u[rows + 1] = stacked(near[0])
@@ -369,26 +366,10 @@
     group_v[0, place] = outgoing(table_y, up_ref[0])
     shared_f = share(group_v.at[0], 2)
 
-    for copies in shared_m:
-        for copy in copies:
-            copy.wait_recv()
-    chains = [jnp.concatenate([eye, eye], axis=0)] * 2
-    for step_index in range(size):
-        for way in range(2):
-            e = step_index if way else size - 1 - step_index
-            mine = place < e if way else place > e
-            high, low = split(jnp.concatenate([jnp.where(mine, chains[way][:80], 0.0), chains[way][80:]], 0))
-            factors[way, e, 0] = high
-            factors[way, e, 1] = low
-            m = group_m[way, e]
-            mh, ml = split(m)
-            full = chains[way][:, :80]
-            ch, cl = split(full)
-            following = mm(ch, mh) + mm(ch, ml) + mm(cl, mh)
-            chains[way] = jnp.concatenate([jnp.where(mine, following[:80], eye), following[80:]], 0)
-    enter = [chain[:80] for chain in chains]
-    state_m[0, 0] = chains[0][80:]
-    state_m[1, 0] = chains[1][80:]
+    for p in range(elements):
+        step(elements - 1 - p, True, table_wb, rows, rows + 1, 1, 6, [zero], [wide_b.at[elements - 1 - p]])
+    group_m[1, place] = outgoing(table_wb, down_ref[0])
+    shared_mb = share(group_m.at[1], 1)
 
     def pass_on(way, k, i, source, target, kind):
         offset = rounds[k][i] * size
@@ -403,14 +384,41 @@
             above if way else below,
         )
 
-    def start_m(k):
+    def start_m(way, k):
         return [
             pass_on(way, k, i, state_m.at[way, k], recv_m.at[way, k, i], way)
             for i in range(len(rounds[k]))
-            for way in range(2)
         ]
 
-    pending = start_m(0) if rounds else []
+    def chain_maps(way, copies):
+        for copy in copies:
+            copy.wait_recv()
+        chain = jnp.concatenate([eye, eye], axis=0)
+        for index in range(size):
+            e = index if way else size - 1 - index
+            mine = place < e if way else place > e
+            high, low = split(jnp.concatenate([jnp.where(mine, chain[:80], 0.0), chain[80:]], 0))
+            factors[way, e, 0] = high
+            factors[way, e, 1] = low
+            following = product(chain[:, :80], group_m[way, e])
+            chain = jnp.concatenate([jnp.where(mine, following[:80], eye), following[80:]], 0)
+        state_m[way, 0] = chain[80:]
+        return chain[:80], start_m(way, 0) if rounds else []
+
+    def finish_maps(way, pending):
+        for k in range(len(rounds)):
+            arrive(pending)
+            if k + 1 < len(rounds):
+                factor = [recv_m[way, k, i] for i in range(len(rounds[k]))]
+                if k > 0:
+                    factor = [state_m[way, k]] + factor
+                total = factor[-1]
+                for item in factor[-2::-1]:
+                    total = product(item[:, :80], total)
+                state_m[way, k + 1] = total
+                pending = start_m(way, k + 1)
+
+    enter_f, pending_f = chain_maps(0, shared_mf)
 
     table_z[rows, :, 0:128] = none
     table_z[rows, :, 128:256] = none
@@ -429,37 +437,35 @@
         )
     back = outgoing(table_z, down_ref[0])
 
-    for k in range(len(rounds)):
-        arrive(pending)
-        if k + 1 < len(rounds):
-            for way in range(2):
-                factor = [recv_m[way, k, i] for i in range(len(rounds[k]))]
-                if k > 0:
-                    factor = [state_m[way, k]] + factor
-                total = factor[-1]
-                for item in factor[-2::-1]:
-                    total = product(item[:, :80], total)
-                state_m[way, k + 1] = total
-            pending = start_m(k + 1)
-
-    def scan(way, copies):
+    def weighted(way, half):
+        total = jnp.zeros((80, 128), F32)
+        for e in range(size):
+            high, low = split(group_v[way, e])
+            fh = factors[way, e, 0, half : half + 80, :80]
+            fl = factors[way, e, 1, half : half + 80, :80]
+            total = total + mm(fh, high) + mm(fh, low) + mm(fl, high)
+        return total
+
+    def start_v(way, k):
+        return [
+            pass_on(way, k, i, state_v.at[way, k], recv_v.at[way, k, i], 2 + way)
+            for i in range(len(rounds[k]))
+        ]
+
+    def start_scan(way, copies):
         for copy in copies:
             copy.wait_recv()
-        total = jnp.zeros((160, 128), F32)
-        for e in range(size):
-            high, low = split(group_v[way, e])
-            fh, fl = factors[way, e, 0][:, :80], factors[way, e, 1][:, :80]
-            total = total + mm(fh, high) + mm(fh, low) + mm(fl, high)
         if not rounds:
-            return total[:80]
-        state_v[way, 0] = total[80:]
+            return weighted(way, 0), []
+        state_v[way, 0] = weighted(way, 80)
+        moving = start_v(way, 0)
+        return weighted(way, 0), moving
+
+    def finish_scan(way, own, moving, enter):
+        if not rounds:
+            return own
         for k, offsets in enumerate(rounds):
-            arrive(
-                [
-                    pass_on(way, k, i, state_v.at[way, k], recv_v.at[way, k, i], 2 + way)
-                    for i in range(len(offsets))
-                ]
-            )
+            arrive(moving)
             links = [(recv_v.at[way, k, i], recv_m.at[way, k, i]) for i in range(len(offsets))]
             if k > 0:
                 links = [(state_v.at[way, k], state_m.at[way, k])] + links
@@ -467,14 +473,21 @@
             for term, factor in links[-2::-1]:
                 value = term[...] + product(factor[:, :80], value)
             state_v[way, k + 1] = value
-        return total[:80] + product(enter[way][:, :80], state_v[way, len(rounds)])
+            if k + 1 < len(rounds):
+                moving = start_v(way, k + 1)
+        return own + product(enter[:, :80], state_v[way, len(rounds)])
 
     both[...] = jnp.zeros(both.shape, F32)
-    incoming = scan(0, shared_f)
+    own, moving = start_scan(0, shared_f)
+    enter_b, pending_b = chain_maps(1, shared_mb)
+    finish_maps(0, pending_f)
+    incoming = finish_scan(0, own, moving, enter_f)
     group_v[1, place] = back[:, :128] + product(back[:, 128:208], incoming)
     shared_b = share(group_v.at[1], 3)
     both[0:80] = incoming
-    both[128:208] = scan(1, shared_b)
+    finish_maps(1, pending_b)
+    own, moving = start_scan(1, shared_b)
+    both[128:208] = finish_scan(1, own, moving, enter_b)
 
     high, low = split(both[...])
     for j in range(elements):

time: 55.4 us -> 50.1 us (0.904)
  Pallas kernels: 48.4 us -> 43.3 us
    pallas_call x1, Pallas kernels: 48.4 us -> 43.3 us  [on_device(): pl.pallas_call(functools.partial(kernel, curve_size, colour_size), out_sh...]
where the time goes in v2:
time: 50.1 us; the launch traced here: 50 us
  Pallas kernels  43.3 us (86%)
  local copies, waits for them, and re-layouts  5.43 us (11%)
  between operations  1.32 us (3%)
    pallas_call x1, Pallas kernels, on_device(): pl.pallas_call(functools.partial(kernel, curve_size, colour_size), out_sh...  43.3 us
    unnamed x3, local copies, waits for them, and re-layouts  1.97 us
    reshape x2, local copies, waits for them, and re-layouts, on_device(): volume_jac.reshape(elements, 3, 5, 320)  1.74 us
    transpose x1, local copies, waits for them, and re-layouts, on_device(): jnp.transpose(face_jac, (0, 1, 2, 4, 3)).reshape(rows, 80, 5)  1.72 us

profile of v2, /device:TPU:0, one launch (start us, length us, event | category | flops | bytes accessed | tf_op | source)
XLA Modules:
  0.0 50.0 jit_solution(14370833190024063342)
XLA Ops:
  1.3 0.0 copy-start
  1.3 1.0 %copy.17 = f32[4,3,5,5,64]{4,3,2,1,0:T(8,128)S(1)} copy(f32[4,3,5,5,64]{4,0,3,2,1:T(4,128)} %param.14) | data formatting | bytes 153600 | tf_op jit(solution)/shard_map/reshape | solution.py:579
  2.3 0.7 %reshape.8.vjac_ref = f32[4,3,5,320]{3,2,1,0:T(8,128)} reshape(f32[4,3,5,5,64]{4,3,2,1,0:T(8,128)S(1)} %copy.17) | data formatting | bytes 153600 | tf_op jit(solution)/shard_map/reshape | solution.py:579
  3.0 0.0 copy-done
  3.1 1.7 %copy.14 = f32[4,6,5,16,5]{4,3,2,1,0:T(8,128)} copy(f32[4,6,5,16,5]{3,0,4,2,1:T(4,128)S(1)} %bitcast.3) | data formatting | bytes 76800 | tf_op jit(solution)/shard_map/transpose | solution.py:578
  4.8 43.3 %whole.1 = f32[4,320,128]{2,1,0:T(8,128)} custom-call(s32[4,6]{1,0:T(4,128)} %kind_ref.1, s32[4,6]{1,0:T(4,128)} %slot_ref.1, s32[4,6]{1,0:T(4,128)} %hang_ref.1, s32[1]{0:T(128)S(6)} %copy.20.up_ref, s32[1]{0:T(128)S(6)} %copy.21.down_ref, f32[4,320,128]{2,1,0:T(8,128)} %u_ref.1, bf16[4,320,320]{2,1,0:T(8,128)(2,1)} %inv_ref.1, f32[24,80,5]{2,1,0:T(8,128)} %bitcast.2, ...), custom_call_target="tpu_custom_call" | custom-call | tf_op jit(solution)/shard_map/whole/pallas_call | solution.py:529
  48.0 2.0 %copy.22 = f32[4,320,128]{2,1,0:T(8,128)} copy(f32[4,320,128]{2,1,0:T(8,128)} %whole.1) | data formatting | bytes 1310720
Async XLA Ops:
  1.3 1.8 %copy-start = (f32[4,6,5,5,16]{4,0,3,2,1:T(4,128)S(1)}, f32[4,6,5,5,16]{4,0,3,2,1:T(4,128)}, u32[]{:S(2)}) copy-start(f32[4,6,5,5,16]{4,0,3,2,1:T(4,128)} %param.13) | copy-start | bytes 115204

commit v3 on v2

--- a/solution.py
+++ b/solution.py
@@ -262,18 +262,18 @@
     table_u[rows] = none
     leaving[0] = traces[up_ref[0]]
     leaving[1] = traces[down_ref[0]]
+    for j in range(elements):
+        for s in range(6):
+            high, low = split(jac_ref[j * 6 + s])
+            wide = (mm(high, spread) + mm(low, spread)) * mortar_ref[hang_ref[j, s]]
+            high = wide.astype(BF16).astype(F32)
+            maps[j * 6 + s] = jnp.where(lane < 160, high, wide - high).astype(BF16)
     pl.semaphore_wait(barrier, greeted)
     after, before = me + 1 < count, me > 0
     near_copies = [
         remote(leaving.at[0], near.at[0], near_send.at[0], near_recv.at[0], me + 1, after, before),
         remote(leaving.at[1], near.at[1], near_send.at[1], near_recv.at[1], me - 1, before, after),
     ]
-    for j in range(elements):
-        for s in range(6):
-            high, low = split(jac_ref[j * 6 + s])
-            wide = (mm(high, spread) + mm(low, spread)) * mortar_ref[hang_ref[j, s]]
-            high = wide.astype(BF16).astype(F32)
-            maps[j * 6 + s] = jnp.where(lane < 160, high, wide - high).astype(BF16)
 
     def step(j, backward, table, remote_row, empty_row, accs, tmps, own, dests):
         groups = len(dests)
@@ -344,9 +344,6 @@
     group_m[0, place] = outgoing(table_wf, up_ref[0])
     shared_mf = share(group_m.at[0], 0)
 
-    arrive(near_copies)
-    table_u[rows + 1] = stacked(near[0])
-    table_u[rows + 2] = stacked(near[1])
     for j in range(elements):
         parts = []
         for f in range(5):
@@ -356,6 +353,10 @@
             parts.append(part)
         volume = jnp.concatenate(parts, axis=0)
         image[j] = u_ref[j] + product(volume, u_ref[j])
+    arrive(near_copies)
+    table_u[rows + 1] = stacked(near[0])
+    table_u[rows + 2] = stacked(near[1])
+    for j in range(elements):
         for s in range(6):
             kind, slot = kind_ref[j, s], slot_ref[j, s]
             row = jnp.where(kind == 1, slot, jnp.where(kind == 0, rows, rows + kind - 1))

time: 50.1 us -> 48.6 us (0.970)
  Pallas kernels: 43.3 us -> 41.6 us
    pallas_call x1, Pallas kernels: 43.3 us -> 41.6 us  [on_device(): pl.pallas_call(functools.partial(kernel, curve_size, colour_size), out_sh...]
where the time goes in v3:
time: 48.6 us; the launch traced here: 48.4 us
  Pallas kernels  41.6 us (86%)
  local copies, waits for them, and re-layouts  5.43 us (11%)
  between operations  1.32 us (3%)
    pallas_call x1, Pallas kernels, on_device(): pl.pallas_call(functools.partial(kernel, curve_size, colour_size), out_sh...  41.6 us
    unnamed x3, local copies, waits for them, and re-layouts  1.97 us
    reshape x2, local copies, waits for them, and re-layouts, on_device(): volume_jac.reshape(elements, 3, 5, 320)  1.74 us
    transpose x1, local copies, waits for them, and re-layouts, on_device(): jnp.transpose(face_jac, (0, 1, 2, 4, 3)).reshape(rows, 80, 5)  1.72 us

profile of v3, /device:TPU:0, one launch (start us, length us, event | category | flops | bytes accessed | tf_op | source)
XLA Modules:
  0.0 48.4 jit_solution(5183248426611408668)
XLA Ops:
  1.3 0.0 copy-start
  1.3 1.0 %copy.17 = f32[4,3,5,5,64]{4,3,2,1,0:T(8,128)S(1)} copy(f32[4,3,5,5,64]{4,0,3,2,1:T(4,128)} %param.14) | data formatting | bytes 153600 | tf_op jit(solution)/shard_map/reshape | solution.py:580
  2.3 0.7 %reshape.8.vjac_ref = f32[4,3,5,320]{3,2,1,0:T(8,128)} reshape(f32[4,3,5,5,64]{4,3,2,1,0:T(8,128)S(1)} %copy.17) | data formatting | bytes 153600 | tf_op jit(solution)/shard_map/reshape | solution.py:580
  3.0 0.0 copy-done
  3.1 1.7 %copy.14 = f32[4,6,5,16,5]{4,3,2,1,0:T(8,128)} copy(f32[4,6,5,16,5]{3,0,4,2,1:T(4,128)S(1)} %bitcast.3) | data formatting | bytes 76800 | tf_op jit(solution)/shard_map/transpose | solution.py:579
  4.8 41.6 %whole.1 = f32[4,320,128]{2,1,0:T(8,128)} custom-call(s32[4,6]{1,0:T(4,128)} %kind_ref.1, s32[4,6]{1,0:T(4,128)} %slot_ref.1, s32[4,6]{1,0:T(4,128)} %hang_ref.1, s32[1]{0:T(128)S(6)} %copy.20.up_ref, s32[1]{0:T(128)S(6)} %copy.21.down_ref, f32[4,320,128]{2,1,0:T(8,128)} %u_ref.1, bf16[4,320,320]{2,1,0:T(8,128)(2,1)} %inv_ref.1, f32[24,80,5]{2,1,0:T(8,128)} %bitcast.2, ...), custom_call_target="tpu_custom_call" | custom-call | tf_op jit(solution)/shard_map/whole/pallas_call | solution.py:530
  46.4 2.0 %copy.22 = f32[4,320,128]{2,1,0:T(8,128)} copy(f32[4,320,128]{2,1,0:T(8,128)} %whole.1) | data formatting | bytes 1310720
Async XLA Ops:
  1.3 1.8 %copy-start = (f32[4,6,5,5,16]{4,0,3,2,1:T(4,128)S(1)}, f32[4,6,5,5,16]{4,0,3,2,1:T(4,128)}, u32[]{:S(2)}) copy-start(f32[4,6,5,5,16]{4,0,3,2,1:T(4,128)} %param.13) | copy-start | bytes 115204
